TPU v7x, 32 devices: a whole 2x2x4 slice. The times are simulated.
32 devices in a mesh: blk: 4 (over y, core), rep: 8 (over z, x).
Axes of the slice: x: 2, y: 2, z: 4, core: 2. Of those that a mesh axis runs over, the one named last changes fastest.
Arguments:
- grad_out: bfloat16 [4096, 256], P(('blk', 'rep')), may hold values from -6 to 6
- relu_bits: int32 [4096, 256], P(('blk', 'rep')), may hold values 0 or 1
- features: bfloat16 [4096, 256], P(('blk', 'rep')), may hold values from -6 to 6
- weight: bfloat16 [256, 256], replicated, may hold values from -0.375 to 0.375
- tiles: bfloat16 [32, 4, 2, 128, 128], P(('blk', 'rep')), as said below
- tile_rows: int32 [32, 4, 2], P(('blk', 'rep')), may hold values from 0 to 7
- tile_counts: int32 [32, 4], P(('blk', 'rep')), may hold values from 1 to 2, as said below
Outputs:
- grad_features: bfloat16 [4096, 256], P(('blk', 'rep'))
- grad_weight: float32 [256, 256], replicated
Inputs may be any that keep to these rules, and one draw needn't show every extreme that they name: `tile_counts`: for every sub-block, some source block has exactly 2 nonzero tiles; loads differ between sub-blocks. `tiles`: about one entry in eight of a tile is nonzero.
All inputs are finite; a program needn't handle non-finite values. No bound on the sum of `relu_bits` on one device may be relied on, other than what follows from the above.
Results may differ from a plain program's by a relative error of at most 0.005.
Values may be sent and summed in bfloat16 or wider, within the bound.
A program may use at most 64 MiB of HBM per device.

v0:
```python
import jax
import jax.numpy as jnp
from jax import lax
from jax.sharding import PartitionSpec as P


def from_behind(array, axis, by):
    devices = lax.axis_size(axis)
    return lax.ppermute(array, axis, [(i, (i + by) % devices) for i in range(devices)])


def body(grad_out, relu_bits, features, weight, tiles, tile_rows, tile_counts):
    nblk = lax.axis_size("blk")
    nrep = lax.axis_size("rep")
    my_block = lax.axis_index("blk")
    rows_here = grad_out.shape[0]
    width = grad_out.shape[1]
    tile_height = tiles.shape[4]
    slot_count = tiles.shape[2]
    block_tiles = rows_here * nrep // tile_height
    masked = jnp.where(relu_bits == 1, grad_out, jnp.zeros_like(grad_out))
    slots = jnp.arange(slot_count, dtype=jnp.int32)
    my_tiles = tiles[0]
    my_rows = tile_rows[0]
    my_counts = tile_counts[0]

    def accumulate(partial_value, piece, source):
        tile_set = lax.dynamic_index_in_dim(my_tiles, source, 0, keepdims=False)
        rows_set = lax.dynamic_index_in_dim(my_rows, source, 0, keepdims=False)
        count = lax.dynamic_index_in_dim(my_counts, source, 0, keepdims=False)
        prods = jnp.einsum("krt,rf->ktf", tile_set, piece, preferred_element_type=jnp.float32)
        live = (slots < count)[:, None, None]
        prods = jnp.where(live, prods, jnp.zeros_like(prods))
        return partial_value.at[rows_set].add(prods)

    partial_value = jnp.zeros((block_tiles, tile_height, width), jnp.float32)
    partial_value = accumulate(partial_value, masked, my_block)

    def one_turn(turn, carry):
        partial_value, held = carry
        held = from_behind(held, "blk", 1)
        source = (my_block - turn) % nblk
        return (accumulate(partial_value, held, source), held)

    partial_value, held = lax.fori_loop(1, nblk, one_turn, (partial_value, masked))
    summed = lax.psum_scatter(
        partial_value.reshape(block_tiles * tile_height, width),
        "rep",
        scatter_dimension=0,
        tiled=True,
    )
    aggregated = summed.astype(jnp.bfloat16)
    grad_features = lax.dot_general(
        aggregated, weight, (((1,), (1,)), ((), ())), preferred_element_type=jnp.float32
    ).astype(jnp.bfloat16)
    weight_term = lax.dot_general(
        features, aggregated, (((0,), (0,)), ((), ())), preferred_element_type=jnp.float32
    )
    total_nodes = rows_here * nrep * nblk
    grad_weight = lax.psum(weight_term, ("blk", "rep")) * total_nodes ** (-0.5)
    return (grad_features, grad_weight)


def solution(mesh):
    return jax.shard_map(
        body,
        mesh=mesh,
        in_specs=(
            P(("blk", "rep"), None),
            P(("blk", "rep"), None),
            P(("blk", "rep"), None),
            P(),
            P(("blk", "rep"), None, None, None, None),
            P(("blk", "rep"), None, None),
            P(("blk", "rep"), None),
        ),
        out_specs=(P(("blk", "rep"), None), P()),
        check_vma=False,
    )
```

profile of v0, /device:TPU:0, one launch (start us, length us, event | category | flops | bytes accessed | tf_op | source)
XLA Modules:
  0.0 233.4 jit_solution(499865236234513302)
XLA Ops:
  7.2 0.0 copy-start
  7.2 0.0 reduce-scatter.2.cloned.1.call-start
  7.2 0.0 copy-start.7
  7.2 0.7 copy-done.7
  7.9 0.6 constant_dynamic-slice_fusion
  8.5 0.0 copy-start.6
  8.5 0.7 iota_compare_fusion.1
  9.2 0.0 copy-done.6
  9.2 0.2 dynamic-slice_reduce_fusion
  9.4 0.1 copy.11
  9.5 0.0 copy-start.3
  9.5 0.0 copy-start.5
  9.5 1.2 copy.10
  10.7 0.0 copy-done.3
  10.7 0.0 copy-done.5
  10.7 1.0 convolution_select_fusion.1
  11.8 0.1 broadcast_in_dim.41
  11.8 0.7 scatter_fusion.1
  12.5 14.6 %while.18 = (s32[]{:T(128)}, f32[8,128,256]{2,1,0:T(8,128)S(1)}, bf16[128,256]{1,0:T(8,128)(2,1)S(1)}, s32[]{:T(128)}, s32[4,2]{1,0:T(4,128)S(1)}, /*index=5*/s3...) while((s32[]{:T(128)}, f32[8,128,256]{2,1,0:T(8,128)S(1)}, ...), condition=%wide.region_3.4_spmd.clone, body=%wide.region_1.3_spmd.clone.sunk | while | flops 16908312 | bytes 1573730 | solution.py:45
  12.6 0.5 collective-permute-start
  13.1 0.6 dynamic_slice.64
  13.7 0.6 iota_compare_fusion.3
  14.3 2.6 %collective-permute-done = bf16[128,256]{1,0:T(8,128)(2,1)S(1)} collective-permute-done((bf16[128,256]{1,0:T(8,128)(2,1)S(1)}, bf16[128,256]{1,0:T(8,128)(2,1)S(1)}, u32[]{:S(2)}, u32[]{:S(2)}) %collective-permute-start) | collective-permute-done | bytes 65568 | tf_op jit(solution)/shard_map/while/body/eval_jaxpr/ppermute | solution.py:9
  17.0 0.2 convolution_select_fusion.3
  17.1 0.7 scatter_fusion
  17.9 0.1 collective-permute-start
  18.0 0.6 dynamic_slice.64
  18.6 0.6 iota_compare_fusion.3
  19.3 2.4 %collective-permute-done = bf16[128,256]{1,0:T(8,128)(2,1)S(1)} collective-permute-done((bf16[128,256]{1,0:T(8,128)(2,1)S(1)}, bf16[128,256]{1,0:T(8,128)(2,1)S(1)}, u32[]{:S(2)}, u32[]{:S(2)}) %collective-permute-start) | collective-permute-done | bytes 65568 | tf_op jit(solution)/shard_map/while/body/eval_jaxpr/ppermute | solution.py:9
  21.6 0.2 convolution_select_fusion.3
  21.8 0.7 scatter_fusion
  22.5 0.1 collective-permute-start
  22.6 0.6 dynamic_slice.64
  23.2 0.6 iota_compare_fusion.3
  23.9 2.4 %collective-permute-done = bf16[128,256]{1,0:T(8,128)(2,1)S(1)} collective-permute-done((bf16[128,256]{1,0:T(8,128)(2,1)S(1)}, bf16[128,256]{1,0:T(8,128)(2,1)S(1)}, u32[]{:S(2)}, u32[]{:S(2)}) %collective-permute-start) | collective-permute-done | bytes 65568 | tf_op jit(solution)/shard_map/while/body/eval_jaxpr/ppermute | solution.py:9
  26.3 0.2 convolution_select_fusion.3
  26.4 0.7 scatter_fusion
  27.2 0.0 copy-start.1
  27.2 0.0 copy-start.4
  27.2 1.0 copy-done.1
  28.1 0.0 reduce-scatter.2.cloned.1.call-update
  28.2 0.0 all-reduce.2.cloned.1.call-start
  28.2 65.5 %reduce-scatter.2.cloned.1.call-done = f32[128,256]{1,0:T(8,128)} async-done(((f32[1024,256]{1,0:T(8,128)}), f32[128,256]{1,0:T(8,128)}) %reduce-scatter.2.cloned.1.call-update) | async-done | bytes 131088 | tf_op jit(solution)/shard_map/reduce_scatter | solution.py:46
  93.8 0.0 copy-done.4
  93.8 1.8 convolution_bitcast_fusion
  95.6 0.0 copy-start.2
  95.6 0.0 all-reduce.2.cloned.1.call-update
  95.6 0.0 copy-done
  95.6 0.9 copy-done.2
  96.5 0.8 convolution_convert_fusion
  97.3 127.4 %all-reduce.2.cloned.1.call-done = f32[256,256]{0,1:T(8,128)} async-done(((f32[256,256]{0,1:T(8,128)}), f32[256,256]{0,1:T(8,128)}) %all-reduce.2.cloned.1.call-update) | async-done | bytes 262160 | tf_op jit(solution)/shard_map/psum | solution.py:60
  224.7 1.0 broadcast_multiply_fusion
  225.7 0.8 copy.12
  (8 shorter events, 0.1 us)
Async XLA Ops:
  7.2 88.4 %copy-start = (bf16[256,256]{1,0:T(8,128)(2,1)S(1)}, bf16[256,256]{1,0:T(8,128)(2,1)}, u32[]{:S(2)}) copy-start(bf16[256,256]{1,0:T(8,128)(2,1)} %param.12) | copy-start | bytes 393220
  7.2 86.6 %reduce-scatter.2.cloned.1.call-start = ((), (), s32[]{:S(2)}) async-start(), calls=%async_computation.1 | async-start | bytes 1179648 | tf_op jit(solution)/shard_map/reduce_scatter | solution.py:46
  7.2 0.7 copy-start.7
  8.5 0.7 copy-start.6
  9.5 1.2 copy-start.3
  9.5 1.2 copy-start.5
  12.6 4.4 %collective-permute-start = (bf16[128,256]{1,0:T(8,128)(2,1)S(1)}, bf16[128,256]{1,0:T(8,128)(2,1)S(1)}, u32[]{:S(2)}, u32[]{:S(2)}) collective-permute-start(bf16[128,256]{1,0:T(8,128)(2,1)S(1)} %get-tuple-element.297), channel_id=1, source_target_pairs={{0,8},{8,16},{16,24},{24,0},{1,9},{9,17},{17,25},{25,1},{2,10},{10... | collective-permute-start | bytes 196616 | tf_op jit(solution)/shard_map/while/body/eval_jaxpr/ppermute | solution.py:9
  17.9 3.7 %collective-permute-start = (bf16[128,256]{1,0:T(8,128)(2,1)S(1)}, bf16[128,256]{1,0:T(8,128)(2,1)S(1)}, u32[]{:S(2)}, u32[]{:S(2)}) collective-permute-start(bf16[128,256]{1,0:T(8,128)(2,1)S(1)} %get-tuple-element.297), channel_id=1, source_target_pairs={{0,8},{8,16},{16,24},{24,0},{1,9},{9,17},{17,25},{25,1},{2,10},{10... | collective-permute-start | bytes 196616 | tf_op jit(solution)/shard_map/while/body/eval_jaxpr/ppermute | solution.py:9
  22.5 3.7 %collective-permute-start = (bf16[128,256]{1,0:T(8,128)(2,1)S(1)}, bf16[128,256]{1,0:T(8,128)(2,1)S(1)}, u32[]{:S(2)}, u32[]{:S(2)}) collective-permute-start(bf16[128,256]{1,0:T(8,128)(2,1)S(1)} %get-tuple-element.297), channel_id=1, source_target_pairs={{0,8},{8,16},{16,24},{24,0},{1,9},{9,17},{17,25},{25,1},{2,10},{10... | collective-permute-start | bytes 196616 | tf_op jit(solution)/shard_map/while/body/eval_jaxpr/ppermute | solution.py:9
  27.2 1.0 copy-start.1
  27.2 66.6 %copy-start.4 = (bf16[128,256]{1,0:T(8,128)(2,1)S(1)}, bf16[128,256]{1,0:T(8,128)(2,1)}, u32[]{:S(2)}) copy-start(bf16[128,256]{1,0:T(8,128)(2,1)} %param.11) | copy-start | bytes 196612
  28.2 196.6 %all-reduce.2.cloned.1.call-start = ((), (), s32[]{:S(2)}) async-start(), calls=%async_computation.2 | async-start | bytes 524288 | tf_op jit(solution)/shard_map/psum | solution.py:60
  95.6 0.9 copy-start.2
Sparse Core Ops, SparseCore 0:
  28.3 65.4 reduce-scatter.1
  100.7 123.9 all-reduce.1
where the time goes:
time: 234 us; the launch traced here: 233 us
  waiting for transfers between devices  200 us (85%)
  between operations  14.2 us (6%)
  local copies, waits for them, and re-layouts  7.35 us (3%)
  other arithmetic  6.37 us (3%)
  matrix products  4.2 us (2%)
    psum x1, waiting for transfers between devices, body(): grad_weight = lax.psum(weight_term, ('blk', 'rep')) * total_nodes ** (-0.5)  127 us
    reduce_scatter x1, waiting for transfers between devices, body(): lax.psum_scatter(partial_value.reshape(block_tiles * tile_height, width),...  65.5 us
    ppermute x3, waiting for transfers between devices, from_behind(): lax.ppermute(array, axis, [(i, (i + by) % devices) for i in range(devices)])  7.38 us
  transfers between devices with their start and end apart: 5, of which 5 were waited for; matrix products, arithmetic and copies ran while one was open for 2% of the time, Pallas kernels for 0%

commit v1 on v0

--- a/solution.py
+++ b/solution.py
@@ -1,7 +1,16 @@
+import functools
 import jax
 import jax.numpy as jnp
 from jax import lax
 from jax.sharding import PartitionSpec as P
+
+
+def _replace_tokens(xx, ax_name):
+    r2 = lax.all_gather(xx, axis_name=ax_name)
+    return jnp.sum(r2, axis=0)
+
+
+arrange_sector = functools.partial(_replace_tokens, ax_name=("blk", "rep"))
 
 
 def from_behind(array, axis, by):
@@ -57,7 +66,7 @@
         features, aggregated, (((0,), (0,)), ((), ())), preferred_element_type=jnp.float32
     )
     total_nodes = rows_here * nrep * nblk
-    grad_weight = lax.psum(weight_term, ("blk", "rep")) * total_nodes ** (-0.5)
+    grad_weight = arrange_sector(weight_term) * total_nodes ** (-0.5)
     return (grad_features, grad_weight)
 
 

time: 234 us -> 201 us (0.86)
  waiting for transfers between devices: 200 us -> 154 us
  local copies, waits for them, and re-layouts: 7.35 us -> 16.8 us
    psum x1 -> x0, waiting for transfers between devices: 127 us -> none  [body(): grad_weight = lax.psum(weight_term, ('blk', 'rep')) * total_nodes ** (-0.5)]
    all_gather x0 -> x1, waiting for transfers between devices: none -> 83.9 us  [_replace_tokens(): r2 = lax.all_gather(xx, axis_name=ax_name)]
    unnamed x19 -> x10, local copies, waits for them, and re-layouts: 4.64 us -> 10.6 us
    ppermute x3, waiting for transfers between devices: 7.38 us -> 3.66 us  [from_behind(): lax.ppermute(array, axis, [(i, (i + by) % devices) for i in range(devices)])]
    dynamic_slice x4, local copies, waits for them, and re-layouts: 2.43 us -> 5.3 us  [accumulate(): count = lax.dynamic_index_in_dim(my_counts, source, 0, keepdims=False)]
  transfers between devices with their start and end apart: 5 -> 5, of which waited for: 5 -> 5; matrix products, arithmetic and copies ran while one was open for 2% -> 4% of each run, Pallas kernels for 0% -> 0%
where the time goes in v1:
time: 201 us
  waiting for transfers between devices  154 us (77%)
  local copies, waits for them, and re-layouts  16.8 us (8%)
  between operations  14.1 us (7%)
  other arithmetic  8.5 us (4%)
  matrix products  5.1 us (3%)
  starting transfers between devices  2.21 us (1%)
    all_gather x1, waiting for transfers between devices, _replace_tokens(): r2 = lax.all_gather(xx, axis_name=ax_name)  83.9 us
    reduce_scatter x1, waiting for transfers between devices, body(): lax.psum_scatter(partial_value.reshape(block_tiles * tile_height, width),...  66.1 us
    unnamed x10, local copies, waits for them, and re-layouts  10.6 us
    dynamic_slice x4, local copies, waits for them, and re-layouts, accumulate(): count = lax.dynamic_index_in_dim(my_counts, source, 0, keepdims=False)  5.3 us
  transfers between devices with their start and end apart: 5, of which 5 were waited for; matrix products, arithmetic and copies ran while one was open for 4% of the time, Pallas kernels for 0%

profile of v1, /device:TPU:0, one launch (start us, length us, event | category | flops | bytes accessed | tf_op | source)
XLA Modules:
  0.0 200.6 jit_solution(3365789390521299628)
XLA Ops:
  7.2 0.0 copy-start
  7.2 0.0 copy-start.2
  7.2 0.0 reduce-scatter.2.cloned.1.call-start
  7.2 1.4 constant_dynamic-slice_fusion
  8.6 0.7 iota_compare_fusion.1
  9.3 0.9 dynamic-slice_reduce_fusion
  10.2 0.8 copy.14
  10.9 1.1 copy.13
  12.1 1.0 compare_select_fusion.1
  13.0 1.0 convolution_select_fusion.1
  14.1 0.1 broadcast_in_dim.41
  14.2 0.7 scatter_fusion.1
  14.9 14.6 %while.18 = (s32[]{:T(128)}, f32[8,128,256]{2,1,0:T(8,128)S(1)}, bf16[128,256]{1,0:T(8,128)(2,1)S(1)}, s32[]{:T(128)}, s32[4,2]{1,0:T(4,128)S(1)}, /*index=5*/s3...) while((s32[]{:T(128)}, f32[8,128,256]{2,1,0:T(8,128)S(1)}, ...), condition=%wide.region_3.4_spmd.clone, body=%wide.region_1.3_spmd.clone.sunk | while | flops 16908312 | bytes 1573730 | solution.py:54
  14.9 0.5 collective-permute-start
  15.4 1.3 dynamic_slice.64
  16.7 0.7 iota_compare_fusion.3
  17.4 1.9 collective-permute-done
  19.3 0.2 convolution_select_fusion.3
  19.5 0.7 scatter_fusion
  20.2 0.8 collective-permute-start
  21.0 1.3 dynamic_slice.64
  22.3 0.7 iota_compare_fusion.3
  23.1 0.9 collective-permute-done
  23.9 0.2 convolution_select_fusion.3
  24.1 0.7 scatter_fusion
  24.8 0.8 collective-permute-start
  25.7 1.3 dynamic_slice.64
  27.0 0.7 iota_compare_fusion.3
  27.7 0.9 collective-permute-done
  28.6 0.2 convolution_select_fusion.3
  28.8 0.7 scatter_fusion
  29.5 0.0 copy-start.1
  29.5 1.0 copy-done.1
  30.5 0.0 reduce-scatter.2.cloned.1.call-update
  30.5 0.0 all-gather.3.cloned.1.call-start
  30.5 66.1 %reduce-scatter.2.cloned.1.call-done = f32[128,256]{1,0:T(8,128)} async-done(((f32[1024,256]{1,0:T(8,128)}), f32[128,256]{1,0:T(8,128)}) %reduce-scatter.2.cloned.1.call-update) | async-done | bytes 131088 | tf_op jit(solution)/shard_map/reduce_scatter | solution.py:55
  96.6 0.0 copy-done.2
  96.6 1.8 convolution_bitcast_fusion
  98.4 0.0 all-gather.3.cloned.1.call-update
  98.5 0.0 copy-done
  98.5 1.7 convolution_convert_fusion
  100.2 83.9 %all-gather.3.cloned.1.call-done = f32[8192,256]{0,1:T(8,128)} async-done(((f32[256,256]{0,1:T(8,128)}), f32[8192,256]{0,1:T(8,128)}) %all-gather.3.cloned.1.call-update) | async-done | bytes 8388624 | tf_op jit(solution)/shard_map/all_gather | solution.py:9
  184.1 6.8 %copy.16 = f32[32,8,32,256]{3,2,1,0:T(8,128)S(1)} copy(f32[32,8,32,256]{3,1,2,0:T(8,128)} %bitcast.47) | data formatting | bytes 16777216
  190.9 1.9 bitcast_reduce_fusion
  192.9 0.8 copy.15
  (8 shorter events, 0.1 us)
Async XLA Ops:
  7.2 91.3 %copy-start = (bf16[256,256]{1,0:T(8,128)(2,1)S(1)}, bf16[256,256]{1,0:T(8,128)(2,1)}, u32[]{:S(2)}) copy-start(bf16[256,256]{1,0:T(8,128)(2,1)} %param.12) | copy-start | bytes 393220
  7.2 89.4 %copy-start.2 = (bf16[128,256]{1,0:T(8,128)(2,1)S(1)}, bf16[128,256]{1,0:T(8,128)(2,1)}, u32[]{:S(2)}) copy-start(bf16[128,256]{1,0:T(8,128)(2,1)} %param.11) | copy-start | bytes 196612
  7.2 89.4 %reduce-scatter.2.cloned.1.call-start = ((), (), s32[]{:S(2)}) async-start(), calls=%async_computation.1 | async-start | bytes 1179648 | tf_op jit(solution)/shard_map/reduce_scatter | solution.py:55
  14.9 4.4 %collective-permute-start = (bf16[128,256]{1,0:T(8,128)(2,1)S(1)}, bf16[128,256]{1,0:T(8,128)(2,1)S(1)}, u32[]{:S(2)}, u32[]{:S(2)}) collective-permute-start(bf16[128,256]{1,0:T(8,128)(2,1)S(1)} %get-tuple-element.304), channel_id=1, source_target_pairs={{0,8},{8,16},{16,24},{24,0},{1,9},{9,17},{17,25},{25,1},{2,10},{10... | collective-permute-start | bytes 196616 | tf_op jit(solution)/shard_map/while/body/eval_jaxpr/ppermute | solution.py:18
  20.2 3.7 %collective-permute-start = (bf16[128,256]{1,0:T(8,128)(2,1)S(1)}, bf16[128,256]{1,0:T(8,128)(2,1)S(1)}, u32[]{:S(2)}, u32[]{:S(2)}) collective-permute-start(bf16[128,256]{1,0:T(8,128)(2,1)S(1)} %get-tuple-element.304), channel_id=1, source_target_pairs={{0,8},{8,16},{16,24},{24,0},{1,9},{9,17},{17,25},{25,1},{2,10},{10... | collective-permute-start | bytes 196616 | tf_op jit(solution)/shard_map/while/body/eval_jaxpr/ppermute | solution.py:18
  24.8 3.7 %collective-permute-start = (bf16[128,256]{1,0:T(8,128)(2,1)S(1)}, bf16[128,256]{1,0:T(8,128)(2,1)S(1)}, u32[]{:S(2)}, u32[]{:S(2)}) collective-permute-start(bf16[128,256]{1,0:T(8,128)(2,1)S(1)} %get-tuple-element.304), channel_id=1, source_target_pairs={{0,8},{8,16},{16,24},{24,0},{1,9},{9,17},{17,25},{25,1},{2,10},{10... | collective-permute-start | bytes 196616 | tf_op jit(solution)/shard_map/while/body/eval_jaxpr/ppermute | solution.py:18
  29.5 1.0 copy-start.1
  30.5 153.6 %all-gather.3.cloned.1.call-start = ((), (), s32[]{:S(2)}) async-start(), calls=%async_computation.2 | async-start | bytes 8650752 | tf_op jit(solution)/shard_map/all_gather | solution.py:9
Sparse Core Ops, SparseCore 0:
  30.6 65.9 reduce-scatter.1
  100.5 83.5 all-gather.2
